TPU v7x, 32 devices: a whole 2x2x4 slice. The times are simulated.
32 devices in a mesh: seq: 8 (over y, x, core), mp: 4 (over z).
Axes of the slice: x: 2, y: 2, z: 4, core: 2. Of those that a mesh axis runs over, the one named last changes fastest.
Arguments:
- tokens: bfloat16 [1024, 4096], P('seq', 'mp'), may hold values from -6 to 6
- w_proj: bfloat16 [4096, 3, 2048], P('seq', None, 'mp'), may hold values from -0.09375 to 0.09375
- short_filter: float32 [3, 3, 2048], P(None, None, 'mp'), may hold values from -3.5 to 3.5
- long_filter: float32 [2048, 1024], P(('mp', 'seq')), may hold values from -0.1875 to 0.1875
- skip_gain: float32 [2048], P('mp'), may hold values from -4 to 4
Outputs:
- gated: bfloat16 [1024, 2048], P('seq', 'mp')
All inputs are finite; a program needn't handle non-finite values.
Results may differ from a plain program's by a relative error of at most 0.012.
Values may be sent and summed in bfloat16 or wider, within the bound.
A program may use at most 64 MiB of HBM per device.

v0:
```python
import math

import jax
import jax.numpy as jnp
import numpy as np
from jax import lax
from jax.sharding import PartitionSpec as P


def shifted(value, axis, steps):
    count = lax.axis_size(axis)
    leading, last = (max(0, -steps), min(count, count - steps))
    return lax.ppermute(value, axis, [(source, source + steps) for source in range(leading, last)])


def transform(real_part, imag_part, orient, filled):
    length = real_part.shape[-1]
    first = math.gcd(length, 64)
    highest = lax.Precision.HIGHEST
    if length <= 64 or first == 1:
        counter = jnp.arange(length, dtype=jnp.int32)
        angles = (
            2.0
            * math.pi
            / length
            * (counter[:, None] * counter[None, :] % length).astype(jnp.float32)
        )
        cosine = jnp.cos(angles)
        sine = jnp.sin(angles)
        new_real = jnp.dot(real_part, cosine, precision=highest) - orient * jnp.dot(
            imag_part, sine, precision=highest
        )
        new_imag = jnp.dot(imag_part, cosine, precision=highest) + orient * jnp.dot(
            real_part, sine, precision=highest
        )
        return (new_real, new_imag)
    second = length // first
    outer = real_part.shape[:-1]
    live = first
    if filled > 0 and filled % second == 0:
        live = filled // second
    real_grid = real_part.reshape(outer + (first, second))[..., :live, :]
    imag_grid = imag_part.reshape(outer + (first, second))[..., :live, :]
    counter = jnp.arange(first, dtype=jnp.int32)
    angles = (
        2.0 * math.pi / first * (counter[:, None] * counter[None, :] % first).astype(jnp.float32)
    )
    cosine = jnp.cos(angles)[:live]
    sine = jnp.sin(angles)[:live]
    section_real = jnp.einsum(
        "...ab,ak->...kb", real_grid, cosine, precision=highest
    ) - orient * jnp.einsum("...ab,ak->...kb", imag_grid, sine, precision=highest)
    section_imag = jnp.einsum(
        "...ab,ak->...kb", imag_grid, cosine, precision=highest
    ) + orient * jnp.einsum("...ab,ak->...kb", real_grid, sine, precision=highest)
    freq_rows = jnp.arange(first, dtype=jnp.int32)[:, None]
    time_cols = jnp.arange(second, dtype=jnp.int32)[None, :]
    twiddle = 2.0 * math.pi / length * (freq_rows * time_cols).astype(jnp.float32)
    twist_cos = jnp.cos(twiddle)
    twist_sin = jnp.sin(twiddle)
    turned_real = section_real * twist_cos - orient * section_imag * twist_sin
    turned_imag = section_imag * twist_cos + orient * section_real * twist_sin
    inner_real, inner_imag = transform(turned_real, turned_imag, orient, 0)
    final_real = jnp.swapaxes(inner_real, -1, -2).reshape(outer + (length,))
    final_imag = jnp.swapaxes(inner_imag, -1, -2).reshape(outer + (length,))
    return (final_real, final_imag)


def mirrored(values):
    return jnp.concatenate([values[:, :1], values[:, :0:-1]], axis=1)


def long_conv(signal, kernel):
    seq_len = signal.shape[-1]
    padded_signal = jnp.pad(signal.astype(jnp.float32), ((0, 0), (0, seq_len)))
    padded_kernel = jnp.pad(kernel, ((0, 0), (0, seq_len)))
    joint_real, joint_imag = transform(padded_signal, padded_kernel, -1.0, seq_len)
    mirror_real = mirrored(joint_real)
    mirror_imag = mirrored(joint_imag)
    signal_real = 0.5 * (joint_real + mirror_real)
    signal_imag = 0.5 * (joint_imag - mirror_imag)
    kernel_real = 0.5 * (joint_imag + mirror_imag)
    kernel_imag = -0.5 * (joint_real - mirror_real)
    prod_real = signal_real * kernel_real - signal_imag * kernel_imag
    prod_imag = signal_real * kernel_imag + signal_imag * kernel_real
    back_real, back_imag = transform(prod_real, prod_imag, 1.0, 0)
    return back_real[:, :seq_len] / (2.0 * seq_len)


def by_weights(tokens, w_proj, short_filter, long_filter, skip_gain):
    rows_dev = tokens.shape[0]
    margin = short_filter.shape[1] - 1
    width = w_proj.shape[2]
    source = lax.all_gather(tokens, "mp", axis=1, tiled=True)
    projected = jnp.einsum(
        "td,dpc->tpc",
        source,
        lax.all_gather(w_proj, "seq", axis=0, tiled=True),
        preferred_element_type=jnp.float32,
    ).astype(jnp.bfloat16)
    tail = shifted(projected[rows_dev - margin :], "seq", 1)
    extended = jnp.concatenate([tail, projected], axis=0).astype(jnp.float32)
    mixed = jnp.zeros((rows_dev, 3, width), jnp.float32)
    for offset in range(margin + 1):
        mixed = (
            mixed
            + short_filter[:, offset, :][None]
            * extended[margin - offset : margin - offset + rows_dev]
        )
    query_rows = mixed[:, 0]
    product = (mixed[:, 1] * mixed[:, 2]).astype(jnp.bfloat16)
    groups = lax.axis_size("seq")
    channel_count = width // groups
    outgoing = product.reshape(rows_dev, groups, channel_count).transpose(1, 2, 0)
    arrived = lax.all_to_all(outgoing, "seq", split_axis=0, concat_axis=2, tiled=True)[0]
    convolved = long_conv(arrived, long_filter).astype(jnp.bfloat16)[None]
    returned = lax.all_to_all(convolved, "seq", split_axis=2, concat_axis=0, tiled=True)
    back_rows = returned.transpose(2, 0, 1).reshape(rows_dev, width)
    result = query_rows * (
        back_rows.astype(jnp.float32) + skip_gain[None, :] * product.astype(jnp.float32)
    )
    return result.astype(jnp.bfloat16)


def split_float(value):
    high = value.astype(jnp.bfloat16)
    low = (value - high.astype(jnp.float32)).astype(jnp.bfloat16)
    return high, low


def dft_tables(length):
    phase = (4 * np.arange(length)[:, None] + 1) * np.arange(length)[None, :] % (4 * length)
    angles = phase * (2.0 * np.pi / (4 * length))
    table = np.concatenate([np.cos(angles), np.sin(angles)], axis=0).astype(np.float32)
    high = table.astype(jnp.bfloat16)
    low = (table - high.astype(np.float32)).astype(jnp.bfloat16)
    return high, low


def matmul_t(left, right):
    return lax.dot_general(
        left, right, (((1,), (1,)), ((), ())), preferred_element_type=jnp.float32
    )


def matmul(left, right):
    return jnp.dot(left, right, preferred_element_type=jnp.float32)


def filter_spectrum(kernel, tables):
    high, low = tables
    count = kernel.shape[0]
    kernel_high, kernel_low = split_float(kernel)
    both = matmul_t(jnp.concatenate([kernel_high, kernel_low], axis=0), high)
    return both[:count] + both[count:] + matmul_t(kernel_high, low)


def dense_conv(signal, spectrum, tables):
    high, low = tables
    count, length = signal.shape
    own = matmul_t(signal, high) + matmul_t(signal, low)
    own_real, own_imag = own[:, :length], own[:, length:]
    real, imag = spectrum[:, :length], spectrum[:, length:]
    prod = jnp.concatenate(
        [own_real * real - own_imag * imag, own_real * imag + own_imag * real], axis=1
    )
    prod_high, prod_low = split_float(prod)
    both = matmul(jnp.concatenate([prod_high, prod_low], axis=0), high)
    return (both[:count] + both[count:] + matmul(prod_high, low)) * (1.0 / length)


def by_tokens(tokens, w_proj, short_filter, long_filter, skip_gain):
    depth, branches, width = w_proj.shape
    groups = lax.axis_size("seq")
    own = width // groups
    length = tokens.shape[0] * groups
    tables = tuple(jnp.asarray(part) for part in dft_tables(length))
    first = lax.axis_index("seq") * own
    taps = lax.dynamic_slice_in_dim(short_filter, first, own, axis=2)
    gain = lax.dynamic_slice_in_dim(skip_gain, first, own, axis=0)
    spectrum = filter_spectrum(long_filter, tables)
    source = lax.all_gather(tokens, "mp", axis=1, tiled=True)
    features = lax.all_to_all(source, "seq", split_axis=1, concat_axis=0, tiled=True)
    partial = lax.dot_general(
        w_proj.reshape(depth, branches * width),
        features,
        (((0,), (1,)), ((), ())),
        preferred_element_type=jnp.float32,
    ).astype(jnp.bfloat16)
    partial = partial.reshape(branches, groups, own, length)
    terms = lax.all_to_all(partial, "seq", split_axis=1, concat_axis=1, tiled=True)
    projected = jnp.sum(terms.astype(jnp.float32), axis=1).astype(jnp.bfloat16)
    margin = short_filter.shape[1] - 1
    padded = jnp.pad(projected.astype(jnp.float32), ((0, 0), (0, 0), (margin, 0)))
    mixed = jnp.zeros((branches, own, length), jnp.float32)
    for offset in range(margin + 1):
        mixed = mixed + taps[:, offset, :, None] * padded[:, :, margin - offset : margin - offset + length]
    product = (mixed[1] * mixed[2]).astype(jnp.bfloat16)
    convolved = dense_conv(product, spectrum, tables).astype(jnp.bfloat16).astype(jnp.float32)
    result = mixed[0] * (convolved + gain[:, None] * product.astype(jnp.float32))
    returned = lax.all_to_all(
        result.astype(jnp.bfloat16), "seq", split_axis=1, concat_axis=0, tiled=True
    )
    return returned.T


def on_device(tokens, w_proj, short_filter, long_filter, skip_gain):
    if tokens.shape[0] < w_proj.shape[0]:
        return by_tokens(tokens, w_proj, short_filter, long_filter, skip_gain)
    return by_weights(tokens, w_proj, short_filter, long_filter, skip_gain)


def solution(mesh):
    return jax.shard_map(
        on_device,
        mesh=mesh,
        in_specs=(
            P("seq", "mp"),
            P("seq", None, "mp"),
            P(None, None, "mp"),
            P(("mp", "seq"), None),
            P("mp"),
        ),
        out_specs=P("seq", "mp"),
        check_vma=False,
    )
```

profile of v0, /device:TPU:8, one launch (start us, length us, event | category | flops | bytes accessed | tf_op | source)
XLA Modules:
  0.0 129.9 jit_solution(2442107587549159840)
XLA Ops:
  6.5 1.8 %copy.18 = bf16[128,1024]{0,1:T(8,128)(2,1)} copy(bf16[128,1024]{1,0:T(8,128)(2,1)} %param.7) | data formatting | bytes 524288 | tf_op args[0]
  8.4 29.6 %all-gather.2.cloned.1.call-done = bf16[128,4096]{0,1:T(8,128)(2,1)} async-done(((bf16[128,1024]{0,1:T(8,128)(2,1)}), bf16[128,4096]{0,1:T(8,128)(2,1)}) %all-gather.2.cloned.1.call-update) | async-done | bytes 1048592 | tf_op jit(solution)/shard_map/all_gather | solution.py:182
  38.0 3.7 %all-to-all-start = ((bf16[128,8,512]{0,2,1:T(8,128)(2,1)}), bf16[128,8,512]{0,2,1:T(8,128)(2,1)S(1)}, u32[]{:S(2)}, u32[]{:S(2)}) async-start(bf16[128,8,512]{0,2,1:T(8,128)(2,1)} %bitcast.46), calls=%async_computation | async-start | bytes 2097152 | tf_op jit(solution)/shard_map/all_to_all | solution.py:183
  41.7 1.7 %copy.17 = bf16[512,3,512]{0,2,1:T(8,128)(2,1)S(1)} copy(bf16[512,3,512]{2,0,1:T(8,128)(2,1)} %param.8) | data formatting | bytes 3145728 | tf_op args[1]
  43.4 13.7 %all-to-all-done = bf16[128,8,512]{0,2,1:T(8,128)(2,1)S(1)} async-done(((bf16[128,8,512]{0,2,1:T(8,128)(2,1)}), bf16[128,8,512]{0,2,1:T(8,128)(2,1)S(1)}, u32[]{:S(2)}, u32[]{:S(2)}) %all-to-all-start) | async-done | bytes 1048608 | tf_op jit(solution)/shard_map/all_to_all | solution.py:183
  57.1 1.3 %copy.19 = bf16[8,128,512]{2,1,0:T(8,128)(2,1)} copy(bf16[8,128,512]{1,2,0:T(8,128)(2,1)S(1)} %bitcast.43) | data formatting | bytes 2097152 | tf_op jit(solution)/shard_map/all_to_all | solution.py:183
  58.4 3.1 %convolution_convert_fusion = bf16[1536,1024]{1,0:T(8,128)(2,1)S(1)} fusion(bf16[512,1536]{0,1:T(8,128)(2,1)S(1)} %bitcast.45, bf16[1024,512]{1,0:T(8,128)(2,1)} %bitcast.47), kind=kOutput, calls=%fused_computation | convolution fusion | flops 1612185600 | bytes 5767168 | tf_op jit(solution)/shard_map/dot_general | solution.py:184
  61.4 2.1 %copy.20 = bf16[3,8,64,1024]{3,2,0,1:T(8,128)(2,1)} copy(bf16[3,8,64,1024]{3,2,1,0:T(8,128)(2,1)S(1)} %bitcast.44) | data formatting | bytes 6291456 | tf_op jit(solution)/shard_map/reshape | solution.py:190
  63.6 3.8 %all-to-all-start.1 = ((bf16[3,8,64,1024]{3,2,0,1:T(8,128)(2,1)}), bf16[3,8,64,1024]{3,2,0,1:T(8,128)(2,1)S(1)}, u32[]{:S(2)}, u32[]{:S(2)}) async-start(bf16[3,8,64,1024]{3,2,0,1:T(8,128)(2,1)} %copy.20), calls=%async_computation.1 | async-start | bytes 6291456 | tf_op jit(solution)/shard_map/all_to_all | solution.py:191
  67.4 1.0 constant_dynamic-slice_fusion.1
  68.3 1.0 dynamic_slice.7
  69.3 3.7 %fusion.15 = f32[128,2048]{1,0:T(8,128)S(1)} fusion(bf16[2048,1024]{1,0:T(8,128)(2,1)} %constant.23.clone, bf16[64,1024]{1,0:T(8,128)(2,1)S(1)} %get-tuple-element.5, bf16[64,1024]{1,0:T(8,128)(2,1)S(1)} %get-tuple-element.6), kind=kOutput, calls=%fused_computation.32 | convolution fusion | flops 537395200 | bytes 5505024 | tf_op jit(solution)/shard_map/dot_general | solution.py:141
  73.1 2.2 %fusion = f32[64,2048]{1,0:T(8,128)} fusion(bf16[2048,1024]{1,0:T(8,128)(2,1)S(1)} %copy-done, bf16[64,1024]{1,0:T(8,128)(2,1)S(1)} %get-tuple-element.6, f32[128,2048]{1,0:T(8,128)S(1)} %fusion.15), kind=kOutput, calls=%fused_computation.3 | convolution fusion | flops 268697600 | bytes 5898240 | tf_op jit(solution)/shard_map/dot_general | solution.py:141
  75.3 29.9 %all-to-all-done.1 = bf16[3,8,64,1024]{3,2,0,1:T(8,128)(2,1)S(1)} async-done(((bf16[3,8,64,1024]{3,2,0,1:T(8,128)(2,1)}), bf16[3,8,64,1024]{3,2,0,1:T(8,128)(2,1)S(1)}, u32[]{:S(2)}, u32[]{:S(2)}) %all-to-all-start.1) | async-done | bytes 3145760 | tf_op jit(solution)/shard_map/all_to_all | solution.py:191
  105.2 0.6 reduce_sum.12
  105.8 0.1 convert_element_type.47
  105.9 0.6 fusion.10
  106.5 3.9 %fusion.20 = f32[64,2048]{1,0:T(8,128)S(1)} fusion(bf16[64,1024]{1,0:T(8,128)(2,1)S(1)} %fusion.16, bf16[2048,1024]{1,0:T(8,128)(2,1)} %constant.23.clone), kind=kOutput, calls=%fused_computation.43 | convolution fusion | flops 268435456 | bytes 4849664 | tf_op jit(solution)/shard_map/dot_general | solution.py:141
  110.5 1.4 %convolution_add_fusion = f32[64,2048]{1,0:T(8,128)S(1)} fusion(f32[64,2048]{1,0:T(8,128)S(1)} %fusion.20, bf16[64,1024]{1,0:T(8,128)(2,1)S(1)} %fusion.16, bf16[2048,1024]{1,0:T(8,128)(2,1)S(1)} %copy-done.1), kind=kOutput, calls=%fused_computation.1 | convolution fusion | flops 268566528 | bytes 5373952 | tf_op jit(solution)/shard_map/dot_general | solution.py:141
  112.0 0.6 copy-done.2
  112.7 0.7 fusion.12
  113.4 0.9 fusion.7
  114.4 7.9 %all_to_all.43 = bf16[64,8,128]{2,0,1:T(8,128)(2,1)S(1)} all-to-all(bf16[64,8,128]{2,0,1:T(8,128)(2,1)S(1)} %bitcast.48), channel_id=1, replica_groups=mesh['seq'=8,'mp'=4] {'seq'}, dimensions={1} | all-to-all | bytes 262144 | tf_op jit(solution)/shard_map/all_to_all | solution.py:201
  122.3 0.8 copy.22
  (19 shorter events, 0.3 us)
Async XLA Ops:
  6.5 31.5 %all-gather.2.cloned.1.call-start = ((), (), s32[]{:S(2)}) async-start(), calls=%async_computation.3 | async-start | bytes 1310720 | tf_op jit(solution)/shard_map/all_gather | solution.py:182
  38.0 19.1 %all-to-all-start = ((bf16[128,8,512]{0,2,1:T(8,128)(2,1)}), bf16[128,8,512]{0,2,1:T(8,128)(2,1)S(1)}, u32[]{:S(2)}, u32[]{:S(2)}) async-start(bf16[128,8,512]{0,2,1:T(8,128)(2,1)} %bitcast.46), calls=%async_computation | async-start | bytes 2097152 | tf_op jit(solution)/shard_map/all_to_all | solution.py:183
  63.5 5.8 %copy-start.4 = (f32[64,1024]{1,0:T(8,128)S(1)}, f32[64,1024]{1,0:T(8,128)}, u32[]{:S(2)}) copy-start(f32[64,1024]{1,0:T(8,128)} %param.10) | copy-start | bytes 786436
  63.6 41.6 %all-to-all-start.1 = ((bf16[3,8,64,1024]{3,2,0,1:T(8,128)(2,1)}), bf16[3,8,64,1024]{3,2,0,1:T(8,128)(2,1)S(1)}, u32[]{:S(2)}, u32[]{:S(2)}) async-start(bf16[3,8,64,1024]{3,2,0,1:T(8,128)(2,1)} %copy.20), calls=%async_computation.1 | async-start | bytes 6291456 | tf_op jit(solution)/shard_map/all_to_all | solution.py:191
  67.3 5.7 %copy-start = (bf16[2048,1024]{1,0:T(8,128)(2,1)S(1)}, bf16[2048,1024]{1,0:T(8,128)(2,1)}, u32[]{:S(2)}) copy-start(bf16[2048,1024]{1,0:T(8,128)(2,1)} %constant.24.clone) | copy-start | bytes 12582916
  105.8 4.7 %copy-start.1 = (bf16[2048,1024]{1,0:T(8,128)(2,1)S(1)}, bf16[2048,1024]{1,0:T(8,128)(2,1)}, u32[]{:S(2)}) copy-start(bf16[2048,1024]{1,0:T(8,128)(2,1)} %constant.24.clone) | copy-start | bytes 12582916
  106.5 5.4 %copy-start.3 = (f32[64,2048]{1,0:T(8,128)S(1)}, f32[64,2048]{1,0:T(8,128)}, u32[]{:S(2)}) copy-start(f32[64,2048]{1,0:T(8,128)} %fusion) | copy-start | bytes 1572868
  110.5 2.2 %copy-start.2 = (bf16[2048,1024]{1,0:T(8,128)(2,1)S(1)}, bf16[2048,1024]{1,0:T(8,128)(2,1)}, u32[]{:S(2)}) copy-start(bf16[2048,1024]{1,0:T(8,128)(2,1)} %constant.23.clone) | copy-start | bytes 12582916
Sparse Core Ops, SparseCore 0:
  8.9 29.0 all-gather.1
where the time goes:
time: 132 us; the launch traced here: 130 us
  waiting for transfers between devices  73.2 us (55%)
  matrix products  16 us (12%)
  between operations  13.6 us (10%)
  local copies, waits for them, and re-layouts  10.3 us (8%)
  blocking collectives  7.92 us (6%)
  starting transfers between devices  7.44 us (6%)
  other arithmetic  1.47 us (1%)
    all_to_all x1, waiting for transfers between devices, by_tokens(): lax.all_to_all(partial, 'seq', split_axis=1, concat_axis=1, tiled=True)  29.9 us
    all_gather x1, waiting for transfers between devices, by_tokens(): source = lax.all_gather(tokens, 'mp', axis=1, tiled=True)  29.6 us
    all_to_all x1, waiting for transfers between devices, by_tokens(): lax.all_to_all(source, 'seq', split_axis=1, concat_axis=0, tiled=True)  13.7 us
    dot_general x4, matrix products, matmul_t(): lax.dot_general(left, right, (((1,), (1,)), ((), ())), preferred_element_...  11.3 us
    all_to_all x1, blocking collectives, by_tokens(): lax.all_to_all(result.astype(jnp.bfloat16), 'seq', split_axis=1, concat_a...  7.92 us
    unnamed x14, local copies, waits for them, and re-layouts  4.16 us
    all_to_all x1, starting transfers between devices, by_tokens(): lax.all_to_all(partial, 'seq', split_axis=1, concat_axis=1, tiled=True)  3.78 us
    all_to_all x1, starting transfers between devices, by_tokens(): lax.all_to_all(source, 'seq', split_axis=1, concat_axis=0, tiled=True)  3.65 us
  transfers between devices with their start and end apart: 3, of which 3 were waited for; matrix products, arithmetic and copies ran while one was open for 7% of the time, Pallas kernels for 0%

commit v1 on v0

--- a/solution.py
+++ b/solution.py
@@ -4,6 +4,8 @@
 import jax.numpy as jnp
 import numpy as np
 from jax import lax
+from jax.experimental import pallas as pl
+from jax.experimental.pallas import tpu as pltpu
 from jax.sharding import PartitionSpec as P
 
 
@@ -169,6 +171,238 @@
     return (both[:count] + both[count:] + matmul(prod_high, low)) * (1.0 / length)
 
 
+MESH = pl.DeviceIdType.MESH
+
+
+def project_kernel(
+    planes,
+    chips,
+    branches,
+    tokens,
+    weights,
+    out,
+    gathered,
+    features,
+    packed,
+    paired,
+    partial,
+    arrived,
+    z_send,
+    z_recv,
+    f_send,
+    f_recv,
+    p_send,
+    p_recv,
+    w_send,
+    w_recv,
+    r_send,
+    r_recv,
+    own_sem,
+):
+    place = lax.axis_index("seq")
+    plane = lax.axis_index("mp")
+    chip, core = place // 2, lax.rem(place, 2)
+    rows, depth = tokens.shape[0], weights.shape[0]
+    width = weights.shape[1] // branches
+    own = width // (2 * chips)
+    sibling = (chip * 2 + 1 - core, plane)
+
+    barrier = pltpu.get_barrier_semaphore()
+    partners = [(place, lax.rem(plane + step, planes)) for step in range(1, planes)]
+    partners += [(lax.rem(chip + step, chips) * 2 + core, plane) for step in range(1, chips)]
+    partners += [sibling]
+    for partner in partners:
+        pl.semaphore_signal(barrier, inc=1, device_id=partner, device_id_type=MESH)
+    pl.semaphore_wait(barrier, len(partners))
+
+    def remote(source, target, send, recv, device):
+        return pltpu.make_async_remote_copy(
+            src_ref=source,
+            dst_ref=target,
+            send_sem=send,
+            recv_sem=recv,
+            device_id=device,
+            device_id_type=MESH,
+        )
+
+    z_copies = []
+    for step in range(1, planes):
+        copy = remote(
+            tokens,
+            gathered.at[plane],
+            z_send.at[step],
+            z_recv.at[plane],
+            (place, lax.rem(plane + step, planes)),
+        )
+        copy.start()
+        z_copies.append(copy)
+    gathered[plane] = tokens[...]
+
+    def scatter(step):
+        slot = lax.rem(plane - step + planes, planes)
+        if step:
+            remote(
+                tokens, gathered.at[slot], z_send.at[step], z_recv.at[slot], (place, slot)
+            ).wait_recv()
+
+        @pl.when(slot == chip)
+        def _():
+            pltpu.make_async_copy(gathered.at[slot], features.at[place], own_sem).start()
+
+        @pl.when(slot != chip)
+        def _():
+            remote(
+                gathered.at[slot],
+                features.at[place],
+                f_send.at[step],
+                f_recv.at[chip],
+                (slot * 2 + core, plane),
+            ).start()
+
+    scatter(0)
+
+    for branch in range(branches):
+        turned = weights[:, branch * width : (branch + 1) * width].T
+        for group in range(2 * chips):
+            packed[group % 2, group // 2, branch * own : (branch + 1) * own, :] = turned[
+                group * own : (group + 1) * own
+            ]
+    w_copy = remote(packed.at[1 - core], paired, w_send, w_recv, sibling)
+    w_copy.start()
+
+    for step in range(1, planes):
+        scatter(step)
+
+    p_copies = []
+    for step in range(chips):
+        source = lax.rem(chip + step, chips)
+        piece = features.at[source * 2 + core]
+        if step == 0:
+            pltpu.make_async_copy(gathered.at[chip], piece, own_sem).wait()
+        else:
+            remote(
+                gathered.at[0], piece, f_send.at[0], f_recv.at[source], (source * 2 + core, plane)
+            ).wait_recv()
+        copy = remote(piece, piece, p_send.at[step], p_recv.at[source], sibling)
+        copy.start()
+        p_copies.append(copy)
+    w_copy.wait_recv()
+    for step in range(chips):
+        source = lax.rem(chip + step, chips)
+        piece = features.at[source * 2 + 1 - core]
+        remote(piece, piece, p_send.at[step], p_recv.at[source], sibling).wait_recv()
+
+    here = pl.ds(pl.multiple_of(core * depth, depth), depth)
+    there = pl.ds(pl.multiple_of((1 - core) * depth, depth), depth)
+    span = 2
+
+    def product(target, block):
+        near = features[pl.ds(block * span, span), :, here].reshape(span * rows, depth)
+        far = features[pl.ds(block * span, span), :, there].reshape(span * rows, depth)
+        return matmul_t(packed[core, target], near) + matmul_t(paired[target], far)
+
+    blocks = 2 * chips // span
+    r_copies = []
+    for step in list(range(1, chips)):
+        target = lax.rem(chip + step, chips)
+
+        def fill(block, carry, target=target, step=step):
+            columns = pl.ds(pl.multiple_of(block * span * rows, span * rows), span * rows)
+            partial[step - 1, :, columns] = product(target, block).astype(jnp.bfloat16)
+            return carry
+
+        lax.fori_loop(0, blocks, fill, 0)
+        copy = remote(
+            partial.at[step - 1],
+            arrived.at[step - 1],
+            r_send.at[step - 1],
+            r_recv.at[step - 1],
+            (target * 2 + core, plane),
+        )
+        copy.start()
+        r_copies.append(copy)
+
+    def mine(block, carry):
+        columns = pl.ds(pl.multiple_of(block * span * rows, span * rows), span * rows)
+        total[:, columns] = product(chip, block)
+        return carry
+
+    total = out[1]
+    lax.fori_loop(0, blocks, mine, 0)
+    for copy in r_copies:
+        copy.wait_recv()
+
+    def add(block, carry):
+        columns = pl.ds(pl.multiple_of(block * span * rows, span * rows), span * rows)
+        value = total[:, columns]
+        for step in range(chips - 1):
+            value = value + arrived[step, :, columns].astype(jnp.float32)
+        out[0][:, columns] = value.astype(jnp.bfloat16)
+        return carry
+
+    lax.fori_loop(0, blocks, add, 0)
+
+    for copy in z_copies + p_copies + [w_copy] + r_copies:
+        copy.wait_send()
+    for step in range(planes):
+        slot = lax.rem(plane - step + planes, planes)
+
+        @pl.when(slot != chip)
+        def _():
+            remote(
+                gathered.at[slot],
+                features.at[place],
+                f_send.at[step],
+                f_recv.at[chip],
+                (slot * 2 + core, plane),
+            ).wait_send()
+
+
+def projected_channels(tokens, w_proj):
+    depth, branches, width = w_proj.shape
+    rows, wide = tokens.shape
+    groups, planes = lax.axis_size("seq"), lax.axis_size("mp")
+    chips = groups // 2
+    own = width // groups
+    length = rows * groups
+    dma = pltpu.SemaphoreType.DMA
+
+    def body(tokens_ref, weights_ref, out_ref, total_ref, *rest):
+        project_kernel(planes, chips, branches, tokens_ref, weights_ref, (out_ref, total_ref), *rest)
+
+    vmem = pl.BlockSpec(memory_space=pltpu.VMEM)
+    half = jnp.bfloat16
+    return pl.pallas_call(
+        body,
+        out_shape=jax.ShapeDtypeStruct((branches * own, length), half),
+        in_specs=[vmem, vmem],
+        out_specs=vmem,
+        scratch_shapes=[
+            pltpu.VMEM((branches * own, length), jnp.float32),
+            pltpu.VMEM((planes, rows, wide), half),
+            pltpu.VMEM((groups, rows, wide), half),
+            pltpu.VMEM((2, chips, branches * own, depth), half),
+            pltpu.VMEM((chips, branches * own, depth), half),
+            pltpu.VMEM((chips - 1, branches * own, length), half),
+            pltpu.VMEM((chips - 1, branches * own, length), half),
+            dma((planes,)),
+            dma((planes,)),
+            dma((planes,)),
+            dma((chips,)),
+            dma((chips,)),
+            dma((chips,)),
+            dma,
+            dma,
+            dma((chips - 1,)),
+            dma((chips - 1,)),
+            dma,
+        ],
+        compiler_params=pltpu.CompilerParams(
+            collective_id=0, has_side_effects=True, vmem_limit_bytes=48 * 1024 * 1024
+        ),
+    )(tokens, w_proj.reshape(depth, branches * width))
+
+
 def by_tokens(tokens, w_proj, short_filter, long_filter, skip_gain):
     depth, branches, width = w_proj.shape
     groups = lax.axis_size("seq")
@@ -179,17 +413,7 @@
     taps = lax.dynamic_slice_in_dim(short_filter, first, own, axis=2)
     gain = lax.dynamic_slice_in_dim(skip_gain, first, own, axis=0)
     spectrum = filter_spectrum(long_filter, tables)
-    source = lax.all_gather(tokens, "mp", axis=1, tiled=True)
-    features = lax.all_to_all(source, "seq", split_axis=1, concat_axis=0, tiled=True)
-    partial = lax.dot_general(
-        w_proj.reshape(depth, branches * width),
-        features,
-        (((0,), (1,)), ((), ())),
-        preferred_element_type=jnp.float32,
-    ).astype(jnp.bfloat16)
-    partial = partial.reshape(branches, groups, own, length)
-    terms = lax.all_to_all(partial, "seq", split_axis=1, concat_axis=1, tiled=True)
-    projected = jnp.sum(terms.astype(jnp.float32), axis=1).astype(jnp.bfloat16)
+    projected = projected_channels(tokens, w_proj).reshape(branches, own, length)
     margin = short_filter.shape[1] - 1
     padded = jnp.pad(projected.astype(jnp.float32), ((0, 0), (0, 0), (margin, 0)))
     mixed = jnp.zeros((branches, own, length), jnp.float32)
@@ -205,7 +429,9 @@
 
 
 def on_device(tokens, w_proj, short_filter, long_filter, skip_gain):
-    if tokens.shape[0] < w_proj.shape[0]:
+    chips = lax.axis_size("mp")
+    paired = lax.axis_size("seq") == 2 * chips and tokens.shape[1] == 2 * w_proj.shape[0]
+    if paired and tokens.shape[0] < w_proj.shape[0]:
         return by_tokens(tokens, w_proj, short_filter, long_filter, skip_gain)
     return by_weights(tokens, w_proj, short_filter, long_filter, skip_gain)
 

time: 132 us -> 91.8 us (0.70); the launches traced: 130 us -> 91.5 us
  waiting for transfers between devices: 73.2 us -> 0 us
  Pallas kernels: 0 us -> 63.1 us
  between operations: 13.6 us -> 0.17 us
  matrix products: 16 us -> 7.38 us
  starting transfers between devices: 7.44 us -> 0 us
  blocking collectives: 7.92 us -> 15.2 us
  local copies, waits for them, and re-layouts: 10.3 us -> 4.89 us
    pallas_call x0 -> x1, Pallas kernels: none -> 63.1 us  [projected_channels(): pl.pallas_call(body, out_shape=jax.ShapeDtypeStruct((branches * own, leng...]
    all_to_all x2 -> x0, waiting for transfers between devices: 43.5 us -> none  [the longest x1 29.9 us: by_tokens(): lax.all_to_all(partial, 'seq', split_axis=1, concat_axis=1, tiled=True)]
    all_gather x1 -> x0, waiting for transfers between devices: 29.6 us -> none  [by_tokens(): source = lax.all_gather(tokens, 'mp', axis=1, tiled=True)]
    all_to_all x2 -> x0, starting transfers between devices: 7.43 us -> none  [the longest x1 3.78 us: by_tokens(): lax.all_to_all(partial, 'seq', split_axis=1, concat_axis=1, tiled=True)]
    all_to_all x1, blocking collectives: 7.92 us -> 15.2 us  [by_tokens(): lax.all_to_all(result.astype(jnp.bfloat16), 'seq', split_axis=1, concat_a...]
    dot_general x4, matrix products: 11.3 us -> 5.72 us  [matmul_t(): lax.dot_general(left, right, (((1,), (1,)), ((), ())), preferred_element_...]
    dot_general x1 -> x0, matrix products: 3.05 us -> none  [by_tokens(): lax.dot_general(w_proj.reshape(depth, branches * width), features, (((0,)...]
    unnamed x14 -> x11, local copies, waits for them, and re-layouts: 4.16 us -> 1.75 us
  transfers between devices with their start and end apart: 3 -> 0, of which waited for: 3 -> 0; matrix products, arithmetic and copies ran while one was open for 7% -> 0% of each run, Pallas kernels for 0% -> 0%
where the time goes in v1:
time: 91.8 us; the launch traced here: 91.5 us
  Pallas kernels  63.1 us (69%)
  blocking collectives  15.2 us (17%)
  matrix products  7.38 us (8%)
  local copies, waits for them, and re-layouts  4.89 us (5%)
    pallas_call x1, Pallas kernels, projected_channels(): pl.pallas_call(body, out_shape=jax.ShapeDtypeStruct((branches * own, leng...  63.1 us
    all_to_all x1, blocking collectives, by_tokens(): lax.all_to_all(result.astype(jnp.bfloat16), 'seq', split_axis=1, concat_a...  15.2 us
    dot_general x4, matrix products, matmul_t(): lax.dot_general(left, right, (((1,), (1,)), ((), ())), preferred_element_...  5.72 us

profile of v1, /device:TPU:8, one launch (start us, length us, event | category | flops | bytes accessed | tf_op | source)
XLA Modules:
  0.0 91.5 jit_solution(8896108320948547222)
XLA Ops:
  0.0 0.0 copy-start
  0.0 0.9 constant_dynamic-slice_fusion.1
  0.9 1.7 %copy.10 = bf16[512,3,512]{0,2,1:T(8,128)(2,1)S(1)} copy(bf16[512,3,512]{2,0,1:T(8,128)(2,1)} %param.8) | data formatting | bytes 3145728 | tf_op args[1]
  2.6 0.7 copy.11.weights_ref
  3.3 0.0 copy-done
  3.3 0.0 copy-start.3
  3.3 0.0 copy-start.2
  3.4 63.1 %shard_map.73 = bf16[192,1024]{1,0:T(8,128)(2,1)S(1)} custom-call(bf16[128,1024]{1,0:T(8,128)(2,1)S(1)} %copy-done, bf16[512,1536]{1,0:T(8,128)(2,1)S(1)} %copy.11.weights_ref), custom_call_target="tpu_custom_call" | custom-call | tf_op jit(solution)/shard_map/pallas_call | solution.py:375
  66.5 0.0 copy-start.1
  66.5 0.1 convert.1
  66.6 0.6 fusion.10
  67.2 0.0 copy-done.3
  67.2 0.0 copy-done.2
  67.3 1.4 %fusion.20 = f32[64,2048]{1,0:T(8,128)S(1)} fusion(bf16[64,1024]{1,0:T(8,128)(2,1)S(1)} %fusion.16, bf16[2048,1024]{1,0:T(8,128)(2,1)S(1)} %copy-done.2), kind=kOutput, calls=%fused_computation.42 | convolution fusion | flops 268435456 | bytes 4849664 | tf_op jit(solution)/shard_map/dot_general | solution.py:143
  68.6 0.0 copy-done.1
  68.7 1.4 %convolution_add_fusion = f32[64,2048]{1,0:T(8,128)S(1)} fusion(f32[64,2048]{1,0:T(8,128)S(1)} %fusion.20, bf16[64,1024]{1,0:T(8,128)(2,1)S(1)} %fusion.16, bf16[2048,1024]{1,0:T(8,128)(2,1)S(1)} %copy-done.1), kind=kOutput, calls=%fused_computation | convolution fusion | flops 268566528 | bytes 5373952 | tf_op jit(solution)/shard_map/dot_general | solution.py:143
  70.1 1.5 %fusion.15 = f32[128,2048]{1,0:T(8,128)S(1)} fusion(bf16[2048,1024]{1,0:T(8,128)(2,1)S(1)} %copy-done.2, bf16[64,1024]{1,0:T(8,128)(2,1)S(1)} %get-tuple-element.5, bf16[64,1024]{1,0:T(8,128)(2,1)S(1)} %get-tuple-element.6), kind=kOutput, calls=%fused_computation.31 | convolution fusion | flops 537395200 | bytes 5505024 | tf_op jit(solution)/shard_map/dot_general | solution.py:143
  71.6 1.4 %fusion = f32[64,2048]{1,0:T(8,128)S(1)} fusion(bf16[2048,1024]{1,0:T(8,128)(2,1)S(1)} %copy-done.1, bf16[64,1024]{1,0:T(8,128)(2,1)S(1)} %get-tuple-element.6, f32[128,2048]{1,0:T(8,128)S(1)} %fusion.15), kind=kOutput, calls=%fused_computation.2 | convolution fusion | flops 268697600 | bytes 5898240 | tf_op jit(solution)/shard_map/dot_general | solution.py:143
  73.0 0.1 multiply_subtract_fusion
  73.1 0.8 dynamic_slice.7
  73.9 0.7 fusion.12
  74.6 0.9 %fusion.7 = bf16[8,8,8,128]{3,2,1,0:T(8,128)(2,1)S(1)} fusion(bf16[2048,1024]{1,0:T(8,128)(2,1)S(1)} %copy-done.1, f32[128,1024]{1,0:T(8,128)S(1)} %fusion.12, f32[3,64,1024]{2,1,0:T(8,128)S(1)} %fusion.10, bf16[64,1024]{1,0:T(8,128)(2,1)S(1)} %fusion.16, f32[64]{0:T(128)S(1)} %dynamic_slice.7, f32[64,1024]{1,0:T(8,128)S(1)} %get-tuple-element.8, ...), kind=kOutput, calls=%fused_computation.10 | convolution fusion | flops 269615104 | bytes 5767424 | tf_op jit(solution)/shard_map/dot_general | solution.py:149
  75.6 15.2 %all_to_all.19 = bf16[64,8,128]{2,0,1:T(8,128)(2,1)S(1)} all-to-all(bf16[64,8,128]{2,0,1:T(8,128)(2,1)S(1)} %bitcast.41), channel_id=1, replica_groups=mesh['seq'=8,'mp'=4] {'seq'}, dimensions={1} | all-to-all | bytes 262144 | tf_op jit(solution)/shard_map/all_to_all | solution.py:425
  90.8 0.8 copy.13
  (7 shorter events, 0.1 us)
Async XLA Ops:
  0.0 3.3 %copy-start = (bf16[128,1024]{1,0:T(8,128)(2,1)S(1)}, bf16[128,1024]{1,0:T(8,128)(2,1)}, u32[]{:S(2)}) copy-start(bf16[128,1024]{1,0:T(8,128)(2,1)} %tokens_ref.1) | copy-start | bytes 786436
  3.3 63.9 %copy-start.3 = (f32[64,1024]{1,0:T(8,128)S(1)}, f32[64,1024]{1,0:T(8,128)}, u32[]{:S(2)}) copy-start(f32[64,1024]{1,0:T(8,128)} %param.10) | copy-start | bytes 786436
  3.3 63.9 %copy-start.2 = (bf16[2048,1024]{1,0:T(8,128)(2,1)S(1)}, bf16[2048,1024]{1,0:T(8,128)(2,1)}, u32[]{:S(2)}) copy-start(bf16[2048,1024]{1,0:T(8,128)(2,1)} %constant.20.clone) | copy-start | bytes 12582916
  66.5 2.2 %copy-start.1 = (bf16[2048,1024]{1,0:T(8,128)(2,1)S(1)}, bf16[2048,1024]{1,0:T(8,128)(2,1)}, u32[]{:S(2)}) copy-start(bf16[2048,1024]{1,0:T(8,128)(2,1)} %constant.21.clone) | copy-start | bytes 12582916

commit v2 on v1

--- a/solution.py
+++ b/solution.py
@@ -1,3 +1,4 @@
+import functools
 import math
 
 import jax
@@ -172,6 +173,7 @@
 
 
 MESH = pl.DeviceIdType.MESH
+PARTS = 2
 
 
 def project_kernel(
@@ -181,6 +183,7 @@
     tokens,
     weights,
     out,
+    total,
     gathered,
     features,
     packed,
@@ -225,41 +228,64 @@
             device_id_type=MESH,
         )
 
-    z_copies = []
-    for step in range(1, planes):
-        copy = remote(
-            tokens,
-            gathered.at[plane],
-            z_send.at[step],
-            z_recv.at[plane],
-            (place, lax.rem(plane + step, planes)),
-        )
-        copy.start()
-        z_copies.append(copy)
+    share = rows // PARTS
+
+    def cut(ref, part):
+        return ref.at[part * share : (part + 1) * share]
+
+    def along_z(part):
+        copies = []
+        for step in range(1, planes):
+            copy = remote(
+                cut(tokens, part),
+                cut(gathered.at[plane], part),
+                z_send.at[part, step],
+                z_recv.at[part, plane],
+                (place, lax.rem(plane + step, planes)),
+            )
+            copy.start()
+            copies.append(copy)
+        return copies
+
+    z_copies = along_z(0)
     gathered[plane] = tokens[...]
 
-    def scatter(step):
+    def scatter_copy(part, step):
         slot = lax.rem(plane - step + planes, planes)
+        return slot, remote(
+            cut(gathered.at[slot], part),
+            cut(features.at[place], part),
+            f_send.at[part, step],
+            f_recv.at[part, chip],
+            (slot * 2 + core, plane),
+        )
+
+    def own_copy(part):
+        return pltpu.make_async_copy(
+            cut(gathered.at[chip], part), cut(features.at[place], part), own_sem.at[part]
+        )
+
+    def scatter(part, step):
+        slot, copy = scatter_copy(part, step)
         if step:
             remote(
-                tokens, gathered.at[slot], z_send.at[step], z_recv.at[slot], (place, slot)
+                cut(tokens, part),
+                cut(gathered.at[slot], part),
+                z_send.at[part, step],
+                z_recv.at[part, slot],
+                (place, slot),
             ).wait_recv()
 
         @pl.when(slot == chip)
         def _():
-            pltpu.make_async_copy(gathered.at[slot], features.at[place], own_sem).start()
+            own_copy(part).start()
 
         @pl.when(slot != chip)
         def _():
-            remote(
-                gathered.at[slot],
-                features.at[place],
-                f_send.at[step],
-                f_recv.at[chip],
-                (slot * 2 + core, plane),
-            ).start()
-
-    scatter(0)
+            copy.start()
+
+    for part in range(PARTS):
+        scatter(part, 0)
 
     for branch in range(branches):
         turned = weights[:, branch * width : (branch + 1) * width].T
@@ -269,93 +295,116 @@
             ]
     w_copy = remote(packed.at[1 - core], paired, w_send, w_recv, sibling)
     w_copy.start()
-
-    for step in range(1, planes):
-        scatter(step)
-
-    p_copies = []
-    for step in range(chips):
-        source = lax.rem(chip + step, chips)
-        piece = features.at[source * 2 + core]
-        if step == 0:
-            pltpu.make_async_copy(gathered.at[chip], piece, own_sem).wait()
-        else:
-            remote(
-                gathered.at[0], piece, f_send.at[0], f_recv.at[source], (source * 2 + core, plane)
-            ).wait_recv()
-        copy = remote(piece, piece, p_send.at[step], p_recv.at[source], sibling)
-        copy.start()
-        p_copies.append(copy)
-    w_copy.wait_recv()
-    for step in range(chips):
-        source = lax.rem(chip + step, chips)
-        piece = features.at[source * 2 + 1 - core]
-        remote(piece, piece, p_send.at[step], p_recv.at[source], sibling).wait_recv()
-
+    for part in range(1, PARTS):
+        for copy in z_copies[-(planes - 1) :]:
+            copy.wait_send()
+        z_copies += along_z(part)
+
+    p_copies, r_copies = [], []
     here = pl.ds(pl.multiple_of(core * depth, depth), depth)
     there = pl.ds(pl.multiple_of((1 - core) * depth, depth), depth)
-    span = 2
-
-    def product(target, block):
-        near = features[pl.ds(block * span, span), :, here].reshape(span * rows, depth)
-        far = features[pl.ds(block * span, span), :, there].reshape(span * rows, depth)
-        return matmul_t(packed[core, target], near) + matmul_t(paired[target], far)
-
-    blocks = 2 * chips // span
-    r_copies = []
-    for step in list(range(1, chips)):
-        target = lax.rem(chip + step, chips)
-
-        def fill(block, carry, target=target, step=step):
-            columns = pl.ds(pl.multiple_of(block * span * rows, span * rows), span * rows)
-            partial[step - 1, :, columns] = product(target, block).astype(jnp.bfloat16)
-            return carry
-
-        lax.fori_loop(0, blocks, fill, 0)
-        copy = remote(
-            partial.at[step - 1],
-            arrived.at[step - 1],
-            r_send.at[step - 1],
-            r_recv.at[step - 1],
-            (target * 2 + core, plane),
-        )
-        copy.start()
-        r_copies.append(copy)
-
-    def mine(block, carry):
-        columns = pl.ds(pl.multiple_of(block * span * rows, span * rows), span * rows)
-        total[:, columns] = product(chip, block)
-        return carry
-
-    total = out[1]
-    lax.fori_loop(0, blocks, mine, 0)
+
+    def forward(part):
+        for step in range(chips):
+            source = lax.rem(chip + step, chips)
+            piece = cut(features.at[source * 2 + core], part)
+            if step == 0:
+                own_copy(part).wait()
+            else:
+                remote(
+                    cut(gathered.at[0], part),
+                    piece,
+                    f_send.at[part, 0],
+                    f_recv.at[part, source],
+                    (source * 2 + core, plane),
+                ).wait_recv()
+            copy = remote(piece, piece, p_send.at[part, step], p_recv.at[part, source], sibling)
+            copy.start()
+            p_copies.append(copy)
+
+    span = 2 * chips // 2
+    across = span * share
+
+    def push(part):
+        if part == 0:
+            w_copy.wait_recv()
+        for step in range(chips):
+            source = lax.rem(chip + step, chips)
+            piece = cut(features.at[source * 2 + 1 - core], part)
+            remote(piece, piece, p_send.at[part, step], p_recv.at[part, source], sibling).wait_recv()
+
+        def product(target, block):
+            which = (pl.ds(block * span, span), slice(part * share, (part + 1) * share))
+            near = features[(*which, here)].reshape(across, depth)
+            far = features[(*which, there)].reshape(across, depth)
+            return matmul_t(packed[core, target], near) + matmul_t(paired[target], far)
+
+        for step in list(range(1, chips)) + [0]:
+            target = lax.rem(chip + step, chips)
+
+            def fill(block, carry, target=target, step=step):
+                columns = pl.ds(pl.multiple_of(block * across, across), across)
+                value = product(target, block)
+                if step:
+                    partial[part, step - 1, :, columns] = value.astype(jnp.bfloat16)
+                else:
+                    total[part, :, columns] = value
+                return carry
+
+            lax.fori_loop(0, 2, fill, 0)
+            if step:
+                copy = remote(
+                    partial.at[part, step - 1],
+                    arrived.at[part, step - 1],
+                    r_send.at[part, step - 1],
+                    r_recv.at[part, step - 1],
+                    (target * 2 + core, plane),
+                )
+                copy.start()
+                r_copies.append(copy)
+
+    for step in range(1, planes):
+        scatter(0, step)
+    forward(0)
+    for part in range(PARTS):
+        if part + 1 < PARTS:
+            for step in range(1, planes):
+                scatter(part + 1, step)
+        push(part)
+        if part + 1 < PARTS:
+            forward(part + 1)
+
     for copy in r_copies:
         copy.wait_recv()
 
-    def add(block, carry):
-        columns = pl.ds(pl.multiple_of(block * span * rows, span * rows), span * rows)
-        value = total[:, columns]
-        for step in range(chips - 1):
-            value = value + arrived[step, :, columns].astype(jnp.float32)
-        out[0][:, columns] = value.astype(jnp.bfloat16)
+    low = lax.broadcasted_iota(jnp.int32, (out.shape[0], rows), 1) < share
+
+    def add(pair, carry):
+        columns = pl.ds(pl.multiple_of(pair * rows, rows), rows)
+        values = []
+        for part in range(PARTS):
+            value = total[part, :, columns]
+            for step in range(chips - 1):
+                value = value + arrived[part, step, :, columns].astype(jnp.float32)
+            values.append(value)
+        first = jnp.where(low, values[0], pltpu.roll(values[1], share, 1))
+        second = jnp.where(low, pltpu.roll(values[0], share, 1), values[1])
+        at = pl.multiple_of(pair * 2 * rows, 2 * rows)
+        out[:, pl.ds(at, rows)] = first.astype(jnp.bfloat16)
+        out[:, pl.ds(pl.multiple_of(at + rows, rows), rows)] = second.astype(jnp.bfloat16)
         return carry
 
-    lax.fori_loop(0, blocks, add, 0)
-
-    for copy in z_copies + p_copies + [w_copy] + r_copies:
+    lax.fori_loop(0, chips, add, 0)
+
+    for copy in z_copies[-(planes - 1) :] + p_copies + [w_copy] + r_copies:
         copy.wait_send()
-    for step in range(planes):
-        slot = lax.rem(plane - step + planes, planes)
-
-        @pl.when(slot != chip)
-        def _():
-            remote(
-                gathered.at[slot],
-                features.at[place],
-                f_send.at[step],
-                f_recv.at[chip],
-                (slot * 2 + core, plane),
-            ).wait_send()
+    for part in range(PARTS):
+        for step in range(planes):
+            slot, copy = scatter_copy(part, step)
+
+            @pl.when(slot != chip)
+            def _(copy=copy):
+                copy.wait_send()
 
 
 def projected_channels(tokens, w_proj):
@@ -367,35 +416,32 @@
     length = rows * groups
     dma = pltpu.SemaphoreType.DMA
 
-    def body(tokens_ref, weights_ref, out_ref, total_ref, *rest):
-        project_kernel(planes, chips, branches, tokens_ref, weights_ref, (out_ref, total_ref), *rest)
-
     vmem = pl.BlockSpec(memory_space=pltpu.VMEM)
     half = jnp.bfloat16
     return pl.pallas_call(
-        body,
+        functools.partial(project_kernel, planes, chips, branches),
         out_shape=jax.ShapeDtypeStruct((branches * own, length), half),
         in_specs=[vmem, vmem],
         out_specs=vmem,
         scratch_shapes=[
-            pltpu.VMEM((branches * own, length), jnp.float32),
+            pltpu.VMEM((PARTS, branches * own, length // PARTS), jnp.float32),
             pltpu.VMEM((planes, rows, wide), half),
             pltpu.VMEM((groups, rows, wide), half),
             pltpu.VMEM((2, chips, branches * own, depth), half),
             pltpu.VMEM((chips, branches * own, depth), half),
-            pltpu.VMEM((chips - 1, branches * own, length), half),
-            pltpu.VMEM((chips - 1, branches * own, length), half),
-            dma((planes,)),
-            dma((planes,)),
-            dma((planes,)),
-            dma((chips,)),
-            dma((chips,)),
-            dma((chips,)),
+            pltpu.VMEM((PARTS, chips - 1, branches * own, length // PARTS), half),
+            pltpu.VMEM((PARTS, chips - 1, branches * own, length // PARTS), half),
+            dma((PARTS, planes)),
+            dma((PARTS, planes)),
+            dma((PARTS, planes)),
+            dma((PARTS, chips)),
+            dma((PARTS, chips)),
+            dma((PARTS, chips)),
             dma,
             dma,
-            dma((chips - 1,)),
-            dma((chips - 1,)),
-            dma,
+            dma((PARTS, chips - 1)),
+            dma((PARTS, chips - 1)),
+            dma((PARTS,)),
         ],
         compiler_params=pltpu.CompilerParams(
             collective_id=0, has_side_effects=True, vmem_limit_bytes=48 * 1024 * 1024

time: 91.8 us -> 78.8 us (0.86)
  Pallas kernels: 63.1 us -> 52.7 us
  blocking collectives: 15.2 us -> 12.6 us
    pallas_call x1, Pallas kernels: 63.1 us -> 52.7 us  [projected_channels(): pl.pallas_call(functools.partial(project_kernel, planes, chips, branches)...]
    all_to_all x1, blocking collectives: 15.2 us -> 12.6 us  [by_tokens(): lax.all_to_all(result.astype(jnp.bfloat16), 'seq', split_axis=1, concat_a...]
where the time goes in v2:
time: 78.8 us; the launch traced here: 78.6 us
  Pallas kernels  52.7 us (67%)
  blocking collectives  12.6 us (16%)
  matrix products  7.38 us (9%)
  local copies, waits for them, and re-layouts  4.89 us (6%)
  other arithmetic  0.85 us (1%)
    pallas_call x1, Pallas kernels, projected_channels(): pl.pallas_call(functools.partial(project_kernel, planes, chips, branches)...  52.7 us
    all_to_all x1, blocking collectives, by_tokens(): lax.all_to_all(result.astype(jnp.bfloat16), 'seq', split_axis=1, concat_a...  12.6 us
    dot_general x4, matrix products, matmul_t(): lax.dot_general(left, right, (((1,), (1,)), ((), ())), preferred_element_...  5.71 us
    unnamed x11, local copies, waits for them, and re-layouts  1.75 us
    dot_general x2, matrix products, matmul(): return jnp.dot(left, right, preferred_element_type=jnp.float32)  1.67 us

profile of v2, /device:TPU:8, one launch (start us, length us, event | category | flops | bytes accessed | tf_op | source)
XLA Modules:
  0.0 78.6 jit_solution(1881457233407334700)
XLA Ops:
  0.0 0.0 copy-start
  0.0 0.9 %constant_dynamic-slice_fusion.1 = (f32[3,1,64]{2,1,0:T(1,128)S(1)}, f32[3,1,64]{2,1,0:T(1,128)S(1)}, f32[3,1,64]{2,1,0:T(1,128)S(1)}) fusion(f32[3,3,512]{2,1,0:T(4,128)} %param.9, s32[]{:T(128)S(6)} %select_n.4, s32[]{:T(128)S(6)} %add.43, s32[]{:T(128)S(6)} %add.44), kind=kLoop, calls=%fused_computation.38 | loop fusion | bytes 4620 | tf_op jit(solution)/shard_map/slice | solution.py:467
  0.9 1.7 %copy.10 = bf16[512,3,512]{0,2,1:T(8,128)(2,1)S(1)} copy(bf16[512,3,512]{2,0,1:T(8,128)(2,1)} %param.8) | data formatting | bytes 3145728 | tf_op args[1]
  2.6 0.7 copy.11.weights
  3.3 0.0 copy-done
  3.3 0.0 copy-start.3
  3.3 0.0 copy-start.2
  3.4 52.7 %shard_map.73 = bf16[192,1024]{1,0:T(8,128)(2,1)S(1)} custom-call(bf16[128,1024]{1,0:T(8,128)(2,1)S(1)} %copy-done, bf16[512,1536]{1,0:T(8,128)(2,1)S(1)} %copy.11.weights), custom_call_target="tpu_custom_call" | custom-call | tf_op jit(solution)/shard_map/pallas_call | solution.py:421
  56.1 0.0 copy-start.1
  56.1 0.1 convert.1
  56.2 0.6 fusion.10
  56.8 0.0 copy-done.3
  56.8 0.0 copy-done.2
  56.9 1.4 %fusion.20 = f32[64,2048]{1,0:T(8,128)S(1)} fusion(bf16[64,1024]{1,0:T(8,128)(2,1)S(1)} %fusion.16, bf16[2048,1024]{1,0:T(8,128)(2,1)S(1)} %copy-done.2), kind=kOutput, calls=%fused_computation.42 | convolution fusion | flops 268435456 | bytes 4849664 | tf_op jit(solution)/shard_map/dot_general | solution.py:144
  58.3 0.0 copy-done.1
  58.3 1.4 %convolution_add_fusion = f32[64,2048]{1,0:T(8,128)S(1)} fusion(f32[64,2048]{1,0:T(8,128)S(1)} %fusion.20, bf16[64,1024]{1,0:T(8,128)(2,1)S(1)} %fusion.16, bf16[2048,1024]{1,0:T(8,128)(2,1)S(1)} %copy-done.1), kind=kOutput, calls=%fused_computation | convolution fusion | flops 268566528 | bytes 5373952 | tf_op jit(solution)/shard_map/dot_general | solution.py:144
  59.7 1.5 %fusion.15 = f32[128,2048]{1,0:T(8,128)S(1)} fusion(bf16[2048,1024]{1,0:T(8,128)(2,1)S(1)} %copy-done.2, bf16[64,1024]{1,0:T(8,128)(2,1)S(1)} %get-tuple-element.5, bf16[64,1024]{1,0:T(8,128)(2,1)S(1)} %get-tuple-element.6), kind=kOutput, calls=%fused_computation.31 | convolution fusion | flops 537395200 | bytes 5505024 | tf_op jit(solution)/shard_map/dot_general | solution.py:144
  61.2 1.4 %fusion = f32[64,2048]{1,0:T(8,128)S(1)} fusion(bf16[2048,1024]{1,0:T(8,128)(2,1)S(1)} %copy-done.1, bf16[64,1024]{1,0:T(8,128)(2,1)S(1)} %get-tuple-element.6, f32[128,2048]{1,0:T(8,128)S(1)} %fusion.15), kind=kOutput, calls=%fused_computation.2 | convolution fusion | flops 268697600 | bytes 5898240 | tf_op jit(solution)/shard_map/dot_general | solution.py:144
  62.6 0.1 multiply_subtract_fusion
  62.7 0.8 dynamic_slice.7
  63.5 0.7 fusion.12
  64.2 0.9 %fusion.7 = bf16[8,8,8,128]{3,2,1,0:T(8,128)(2,1)S(1)} fusion(bf16[2048,1024]{1,0:T(8,128)(2,1)S(1)} %copy-done.1, f32[128,1024]{1,0:T(8,128)S(1)} %fusion.12, f32[3,64,1024]{2,1,0:T(8,128)S(1)} %fusion.10, bf16[64,1024]{1,0:T(8,128)(2,1)S(1)} %fusion.16, f32[64]{0:T(128)S(1)} %dynamic_slice.7, f32[64,1024]{1,0:T(8,128)S(1)} %get-tuple-element.8, ...), kind=kOutput, calls=%fused_computation.10 | convolution fusion | flops 269615104 | bytes 5767424 | tf_op jit(solution)/shard_map/dot_general | solution.py:150
  65.2 12.6 %all_to_all.19 = bf16[64,8,128]{2,0,1:T(8,128)(2,1)S(1)} all-to-all(bf16[64,8,128]{2,0,1:T(8,128)(2,1)S(1)} %bitcast.41), channel_id=1, replica_groups=mesh['seq'=8,'mp'=4] {'seq'}, dimensions={1} | all-to-all | bytes 262144 | tf_op jit(solution)/shard_map/all_to_all | solution.py:471
  77.8 0.8 copy.13
  (7 shorter events, 0.1 us)
Async XLA Ops:
  0.0 3.3 %copy-start = (bf16[128,1024]{1,0:T(8,128)(2,1)S(1)}, bf16[128,1024]{1,0:T(8,128)(2,1)}, u32[]{:S(2)}) copy-start(bf16[128,1024]{1,0:T(8,128)(2,1)} %tokens.1) | copy-start | bytes 786436
  3.3 53.5 %copy-start.3 = (f32[64,1024]{1,0:T(8,128)S(1)}, f32[64,1024]{1,0:T(8,128)}, u32[]{:S(2)}) copy-start(f32[64,1024]{1,0:T(8,128)} %param.10) | copy-start | bytes 786436
  3.3 53.5 %copy-start.2 = (bf16[2048,1024]{1,0:T(8,128)(2,1)S(1)}, bf16[2048,1024]{1,0:T(8,128)(2,1)}, u32[]{:S(2)}) copy-start(bf16[2048,1024]{1,0:T(8,128)(2,1)} %constant.20.clone) | copy-start | bytes 12582916
  56.1 2.2 %copy-start.1 = (bf16[2048,1024]{1,0:T(8,128)(2,1)S(1)}, bf16[2048,1024]{1,0:T(8,128)(2,1)}, u32[]{:S(2)}) copy-start(bf16[2048,1024]{1,0:T(8,128)(2,1)} %constant.21.clone) | copy-start | bytes 12582916

commit v3 on v2

--- a/solution.py
+++ b/solution.py
@@ -150,28 +150,6 @@
     return jnp.dot(left, right, preferred_element_type=jnp.float32)
 
 
-def filter_spectrum(kernel, tables):
-    high, low = tables
-    count = kernel.shape[0]
-    kernel_high, kernel_low = split_float(kernel)
-    both = matmul_t(jnp.concatenate([kernel_high, kernel_low], axis=0), high)
-    return both[:count] + both[count:] + matmul_t(kernel_high, low)
-
-
-def dense_conv(signal, spectrum, tables):
-    high, low = tables
-    count, length = signal.shape
-    own = matmul_t(signal, high) + matmul_t(signal, low)
-    own_real, own_imag = own[:, :length], own[:, length:]
-    real, imag = spectrum[:, :length], spectrum[:, length:]
-    prod = jnp.concatenate(
-        [own_real * real - own_imag * imag, own_real * imag + own_imag * real], axis=1
-    )
-    prod_high, prod_low = split_float(prod)
-    both = matmul(jnp.concatenate([prod_high, prod_low], axis=0), high)
-    return (both[:count] + both[count:] + matmul(prod_high, low)) * (1.0 / length)
-
-
 MESH = pl.DeviceIdType.MESH
 PARTS = 2
 
@@ -182,7 +160,21 @@
     branches,
     tokens,
     weights,
+    scalars,
+    kernel,
+    high_table,
+    low_table,
     out,
+    high,
+    low,
+    spectrum,
+    projected,
+    spectral,
+    leaving,
+    collected,
+    t_sem,
+    a_send,
+    a_recv,
     total,
     gathered,
     features,
@@ -213,7 +205,7 @@
     barrier = pltpu.get_barrier_semaphore()
     partners = [(place, lax.rem(plane + step, planes)) for step in range(1, planes)]
     partners += [(lax.rem(chip + step, chips) * 2 + core, plane) for step in range(1, chips)]
-    partners += [sibling]
+    partners += [(lax.rem(chip + step, chips) * 2 + 1 - core, plane) for step in range(chips)]
     for partner in partners:
         pl.semaphore_signal(barrier, inc=1, device_id=partner, device_id_type=MESH)
     pl.semaphore_wait(barrier, len(partners))
@@ -229,6 +221,10 @@
         )
 
     share = rows // PARTS
+    table_copies = [
+        pltpu.make_async_copy(high_table, high, t_sem.at[0]),
+        pltpu.make_async_copy(low_table, low, t_sem.at[1]),
+    ]
 
     def cut(ref, part):
         return ref.at[part * share : (part + 1) * share]
@@ -248,6 +244,8 @@
         return copies
 
     z_copies = along_z(0)
+    for copy in table_copies:
+        copy.start()
     gathered[plane] = tokens[...]
 
     def scatter_copy(part, step):
@@ -299,6 +297,21 @@
         for copy in z_copies[-(planes - 1) :]:
             copy.wait_send()
         z_copies += along_z(part)
+
+    for copy in table_copies:
+        copy.wait()
+    length = kernel.shape[1]
+    chunk = 2 * rows
+    kernel_high, kernel_low = split_float(kernel[...])
+    kernel_both = jnp.concatenate([kernel_high, kernel_low], axis=0)
+
+    def transform_filter(block, carry):
+        at = pl.ds(pl.multiple_of(block * chunk, chunk), chunk)
+        both = matmul_t(kernel_both, high[at, :])
+        spectrum[:, at] = both[:own] + both[own:] + matmul_t(kernel_high, low[at, :])
+        return carry
+
+    lax.fori_loop(0, 2 * length // chunk, transform_filter, 0)
 
     p_copies, r_copies = [], []
     here = pl.ds(pl.multiple_of(core * depth, depth), depth)
@@ -377,7 +390,7 @@
     for copy in r_copies:
         copy.wait_recv()
 
-    low = lax.broadcasted_iota(jnp.int32, (out.shape[0], rows), 1) < share
+    left = lax.broadcasted_iota(jnp.int32, (branches * own, rows), 1) < share
 
     def add(pair, carry):
         columns = pl.ds(pl.multiple_of(pair * rows, rows), rows)
@@ -387,16 +400,77 @@
             for step in range(chips - 1):
                 value = value + arrived[part, step, :, columns].astype(jnp.float32)
             values.append(value)
-        first = jnp.where(low, values[0], pltpu.roll(values[1], share, 1))
-        second = jnp.where(low, pltpu.roll(values[0], share, 1), values[1])
+        first = jnp.where(left, values[0], pltpu.roll(values[1], share, 1))
+        second = jnp.where(left, pltpu.roll(values[0], share, 1), values[1])
         at = pl.multiple_of(pair * 2 * rows, 2 * rows)
-        out[:, pl.ds(at, rows)] = first.astype(jnp.bfloat16)
-        out[:, pl.ds(pl.multiple_of(at + rows, rows), rows)] = second.astype(jnp.bfloat16)
+        near, far = pl.ds(at, rows), pl.ds(pl.multiple_of(at + rows, rows), rows)
+        projected[:, near] = first.astype(jnp.bfloat16).astype(jnp.float32)
+        projected[:, far] = second.astype(jnp.bfloat16).astype(jnp.float32)
         return carry
 
     lax.fori_loop(0, chips, add, 0)
 
-    for copy in z_copies[-(planes - 1) :] + p_copies + [w_copy] + r_copies:
+    token = lax.broadcasted_iota(jnp.int32, (own, length), 1)
+    mixed = []
+    for branch in range(branches):
+        at = slice(branch * own, (branch + 1) * own)
+        value = projected[at, :]
+        result = scalars[at, 0:1] * value
+        for offset in range(1, scalars.shape[1] - 1):
+            moved = jnp.where(token >= offset, pltpu.roll(value, offset, 1), 0.0)
+            result = result + scalars[at, offset : offset + 1] * moved
+        mixed.append(result)
+    signal = (mixed[1] * mixed[2]).astype(jnp.bfloat16)
+    gain = scalars[0:own, scalars.shape[1] - 1 :]
+    projected[0:own, :] = mixed[0]
+    projected[own : 2 * own, :] = gain * signal.astype(jnp.float32)
+
+    for block in range(length // chunk):
+        real_at = slice(block * chunk, (block + 1) * chunk)
+        imag_at = slice(length + block * chunk, length + (block + 1) * chunk)
+        own_real = matmul_t(signal, high[real_at, :]) + matmul_t(signal, low[real_at, :])
+        own_imag = matmul_t(signal, high[imag_at, :]) + matmul_t(signal, low[imag_at, :])
+        real, imag = spectrum[:, real_at], spectrum[:, imag_at]
+        for at, value in (
+            (real_at, own_real * real - own_imag * imag),
+            (imag_at, own_real * imag + own_imag * real),
+        ):
+            value_high, value_low = split_float(value)
+            spectral[0:own, at] = value_high
+            spectral[own : 2 * own, at] = value_low
+
+    a_copies = []
+    for step in list(range(1, chips)) + [0]:
+        target = lax.rem(chip + step, chips)
+        at = pl.ds(pl.multiple_of(target * chunk, chunk), chunk)
+        both = matmul(spectral[...], high[:, at])
+        value = both[:own] + both[own:] + matmul(spectral[0:own, :], low[:, at])
+        value = (value * (1.0 / length)).astype(jnp.bfloat16).astype(jnp.float32)
+        value = (projected[0:own, at] * (value + projected[own : 2 * own, at])).astype(jnp.bfloat16)
+        leaving[step, 0] = value[:, :rows]
+        leaving[step, 1] = value[:, rows:]
+        for other in (1, 0):
+            side = core if other == 0 else 1 - core
+            if step == 0 and other == 0:
+                collected[place] = leaving[step, side]
+                continue
+            copy = remote(
+                leaving.at[step, side],
+                collected.at[place],
+                a_send.at[step, other],
+                a_recv.at[place],
+                (target * 2 + side, plane),
+            )
+            copy.start()
+            a_copies.append(copy)
+    for step in range(1, 2 * chips):
+        source = lax.rem(place + step, 2 * chips)
+        remote(
+            leaving.at[0, 0], collected.at[source], a_send.at[0, 0], a_recv.at[source], (source, plane)
+        ).wait_recv()
+    out[...] = collected[...].reshape(2 * chips * own, rows).T
+
+    for copy in z_copies[-(planes - 1) :] + p_copies + [w_copy] + r_copies + a_copies:
         copy.wait_send()
     for part in range(PARTS):
         for step in range(planes):
@@ -407,7 +481,7 @@
                 copy.wait_send()
 
 
-def projected_channels(tokens, w_proj):
+def operator_kernel(tokens, w_proj, scalars, long_filter, tables):
     depth, branches, width = w_proj.shape
     rows, wide = tokens.shape
     groups, planes = lax.axis_size("seq"), lax.axis_size("mp")
@@ -420,10 +494,20 @@
     half = jnp.bfloat16
     return pl.pallas_call(
         functools.partial(project_kernel, planes, chips, branches),
-        out_shape=jax.ShapeDtypeStruct((branches * own, length), half),
-        in_specs=[vmem, vmem],
+        out_shape=jax.ShapeDtypeStruct((rows, width), half),
+        in_specs=[vmem] * 4 + [pl.BlockSpec(memory_space=pl.ANY)] * 2,
         out_specs=vmem,
         scratch_shapes=[
+            pltpu.VMEM((2 * length, length), half),
+            pltpu.VMEM((2 * length, length), half),
+            pltpu.VMEM((own, 2 * length), jnp.float32),
+            pltpu.VMEM((branches * own, length), jnp.float32),
+            pltpu.VMEM((2 * own, 2 * length), half),
+            pltpu.VMEM((chips, 2, own, rows), half),
+            pltpu.VMEM((groups, own, rows), half),
+            dma((2,)),
+            dma((chips, 2)),
+            dma((groups,)),
             pltpu.VMEM((PARTS, branches * own, length // PARTS), jnp.float32),
             pltpu.VMEM((planes, rows, wide), half),
             pltpu.VMEM((groups, rows, wide), half),
@@ -446,32 +530,21 @@
         compiler_params=pltpu.CompilerParams(
             collective_id=0, has_side_effects=True, vmem_limit_bytes=48 * 1024 * 1024
         ),
-    )(tokens, w_proj.reshape(depth, branches * width))
+    )(tokens, w_proj.reshape(depth, branches * width), scalars, long_filter, *tables)
 
 
 def by_tokens(tokens, w_proj, short_filter, long_filter, skip_gain):
-    depth, branches, width = w_proj.shape
+    branches, width = w_proj.shape[1:]
     groups = lax.axis_size("seq")
     own = width // groups
-    length = tokens.shape[0] * groups
-    tables = tuple(jnp.asarray(part) for part in dft_tables(length))
+    tables = tuple(jnp.asarray(part) for part in dft_tables(tokens.shape[0] * groups))
     first = lax.axis_index("seq") * own
-    taps = lax.dynamic_slice_in_dim(short_filter, first, own, axis=2)
-    gain = lax.dynamic_slice_in_dim(skip_gain, first, own, axis=0)
-    spectrum = filter_spectrum(long_filter, tables)
-    projected = projected_channels(tokens, w_proj).reshape(branches, own, length)
-    margin = short_filter.shape[1] - 1
-    padded = jnp.pad(projected.astype(jnp.float32), ((0, 0), (0, 0), (margin, 0)))
-    mixed = jnp.zeros((branches, own, length), jnp.float32)
-    for offset in range(margin + 1):
-        mixed = mixed + taps[:, offset, :, None] * padded[:, :, margin - offset : margin - offset + length]
-    product = (mixed[1] * mixed[2]).astype(jnp.bfloat16)
-    convolved = dense_conv(product, spectrum, tables).astype(jnp.bfloat16).astype(jnp.float32)
-    result = mixed[0] * (convolved + gain[:, None] * product.astype(jnp.float32))
-    returned = lax.all_to_all(
-        result.astype(jnp.bfloat16), "seq", split_axis=1, concat_axis=0, tiled=True
+    scalars = jnp.concatenate(
+        [short_filter, jnp.broadcast_to(skip_gain, (branches, 1, width))], axis=1
     )
-    return returned.T
+    scalars = lax.dynamic_slice_in_dim(scalars, first, own, axis=2)
+    scalars = scalars.transpose(0, 2, 1).reshape(branches * own, -1)
+    return operator_kernel(tokens, w_proj, scalars, long_filter, tables)
 
 
 def on_device(tokens, w_proj, short_filter, long_filter, skip_gain):

time: 78.8 us -> 68.7 us (0.87)
  the two profiles are of different devices: /device:TPU:8 before, /device:TPU:20 now
where the time goes in v3:
time: 68.7 us; the launch traced here: 68.5 us
  Pallas kernels  63.2 us (92%)
  local copies, waits for them, and re-layouts  5.17 us (8%)
    pallas_call x1, Pallas kernels, operator_kernel(): pl.pallas_call(functools.partial(project_kernel, planes, chips, branches)...  63.2 us
    unnamed x10, local copies, waits for them, and re-layouts  3.28 us
    reshape x1, local copies, waits for them, and re-layouts, operator_kernel(): w_proj.reshape(depth, branches * width)  1.77 us

profile of v3, /device:TPU:20, one launch (start us, length us, event | category | flops | bytes accessed | tf_op | source)
XLA Modules:
  0.0 68.5 jit_solution(15400573965625797134)
XLA Ops:
  0.0 2.6 %copy.10 = bf16[512,3,512]{0,2,1:T(8,128)(2,1)} copy(bf16[512,3,512]{2,0,1:T(8,128)(2,1)} %param.8) | data formatting | bytes 3145728 | tf_op args[1]
  2.6 0.0 copy-start.3
  2.6 0.0 copy-start.2
  2.6 0.0 copy-start
  2.6 0.0 copy-start.1
  2.6 1.8 %copy.12.weights = bf16[512,1536]{1,0:T(8,128)(2,1)S(1)} copy(bf16[512,1536]{0,1:T(8,128)(2,1)} %bitcast.5) | data formatting | bytes 3145728 | tf_op jit(solution)/shard_map/reshape | solution.py:533
  4.4 0.0 copy-done.3
  4.4 0.0 copy-done.2
  4.4 0.1 fusion.1
  4.5 0.1 copy.11
  4.6 0.0 copy-done
  4.7 0.0 copy-done.1
  4.7 63.2 %shard_map.73 = bf16[128,512]{1,0:T(8,128)(2,1)S(1)} custom-call(bf16[128,1024]{1,0:T(8,128)(2,1)S(1)} %copy-done, bf16[512,1536]{1,0:T(8,128)(2,1)S(1)} %copy.12.weights, f32[192,4]{1,0:T(8,128)S(1)} %bitcast.4, f32[64,1024]{1,0:T(8,128)S(1)} %copy-done.1, bf16[2048,1024]{1,0:T(8,128)(2,1)} %constant.16.clone.high_table, ...), custom_call_target="tpu_custom_call" | custom-call | tf_op jit(solution)/shard_map/pallas_call | solution.py:495
  67.8 0.7 copy.14
  (1 shorter events, 0.0 us)
Async XLA Ops:
  2.6 1.8 %copy-start.3 = (f32[512]{0:T(512)S(1)}, f32[512]{0:T(512)}, u32[]{:S(2)}) copy-start(f32[512]{0:T(512)} %param.11) | copy-start | bytes 6148
  2.6 1.8 %copy-start.2 = (f32[3,3,512]{2,1,0:T(4,128)S(1)}, f32[3,3,512]{2,1,0:T(4,128)}, u32[]{:S(2)}) copy-start(f32[3,3,512]{2,1,0:T(4,128)} %param.9) | copy-start | bytes 55300
  2.6 2.0 %copy-start = (bf16[128,1024]{1,0:T(8,128)(2,1)S(1)}, bf16[128,1024]{1,0:T(8,128)(2,1)}, u32[]{:S(2)}) copy-start(bf16[128,1024]{1,0:T(8,128)(2,1)} %tokens.1) | copy-start | bytes 786436
  2.6 2.0 %copy-start.1 = (f32[64,1024]{1,0:T(8,128)S(1)}, f32[64,1024]{1,0:T(8,128)}, u32[]{:S(2)}) copy-start(f32[64,1024]{1,0:T(8,128)} %kernel.1) | copy-start | bytes 786436

commit v4 on v3

--- a/solution.py
+++ b/solution.py
@@ -159,12 +159,13 @@
     chips,
     branches,
     tokens,
-    weights,
+    weights_far,
     scalars,
     kernel,
     high_table,
     low_table,
     out,
+    weights,
     high,
     low,
     spectrum,
@@ -197,8 +198,8 @@
     place = lax.axis_index("seq")
     plane = lax.axis_index("mp")
     chip, core = place // 2, lax.rem(place, 2)
-    rows, depth = tokens.shape[0], weights.shape[0]
-    width = weights.shape[1] // branches
+    rows, depth = tokens.shape[0], weights.shape[1]
+    width = weights.shape[2]
     own = width // (2 * chips)
     sibling = (chip * 2 + 1 - core, plane)
 
@@ -221,6 +222,7 @@
         )
 
     share = rows // PARTS
+    weight_copy = pltpu.make_async_copy(weights_far, weights, t_sem.at[2])
     table_copies = [
         pltpu.make_async_copy(high_table, high, t_sem.at[0]),
         pltpu.make_async_copy(low_table, low, t_sem.at[1]),
@@ -244,7 +246,7 @@
         return copies
 
     z_copies = along_z(0)
-    for copy in table_copies:
+    for copy in [weight_copy] + table_copies:
         copy.start()
     gathered[plane] = tokens[...]
 
@@ -285,8 +287,9 @@
     for part in range(PARTS):
         scatter(part, 0)
 
+    weight_copy.wait()
     for branch in range(branches):
-        turned = weights[:, branch * width : (branch + 1) * width].T
+        turned = weights[branch].T
         for group in range(2 * chips):
             packed[group % 2, group // 2, branch * own : (branch + 1) * own, :] = turned[
                 group * own : (group + 1) * own
@@ -491,13 +494,15 @@
     dma = pltpu.SemaphoreType.DMA
 
     vmem = pl.BlockSpec(memory_space=pltpu.VMEM)
+    far = pl.BlockSpec(memory_space=pl.ANY)
     half = jnp.bfloat16
     return pl.pallas_call(
         functools.partial(project_kernel, planes, chips, branches),
         out_shape=jax.ShapeDtypeStruct((rows, width), half),
-        in_specs=[vmem] * 4 + [pl.BlockSpec(memory_space=pl.ANY)] * 2,
+        in_specs=[vmem, far, vmem, vmem, far, far],
         out_specs=vmem,
         scratch_shapes=[
+            pltpu.VMEM((branches, depth, width), half),
             pltpu.VMEM((2 * length, length), half),
             pltpu.VMEM((2 * length, length), half),
             pltpu.VMEM((own, 2 * length), jnp.float32),
@@ -505,7 +510,7 @@
             pltpu.VMEM((2 * own, 2 * length), half),
             pltpu.VMEM((chips, 2, own, rows), half),
             pltpu.VMEM((groups, own, rows), half),
-            dma((2,)),
+            dma((3,)),
             dma((chips, 2)),
             dma((groups,)),
             pltpu.VMEM((PARTS, branches * own, length // PARTS), jnp.float32),
@@ -530,7 +535,7 @@
         compiler_params=pltpu.CompilerParams(
             collective_id=0, has_side_effects=True, vmem_limit_bytes=48 * 1024 * 1024
         ),
-    )(tokens, w_proj.reshape(depth, branches * width), scalars, long_filter, *tables)
+    )(tokens, w_proj.transpose(1, 0, 2), scalars, long_filter, *tables)
 
 
 def by_tokens(tokens, w_proj, short_filter, long_filter, skip_gain):

time: 68.7 us -> 69.3 us (level)
    reshape x1 -> x0, local copies, waits for them, and re-layouts: 1.77 us -> none  [operator_kernel(): w_proj.reshape(depth, branches * width)]
    unnamed x10 -> x7, local copies, waits for them, and re-layouts: 3.28 us -> 3.96 us
where the time goes in v4:
time: 69.3 us; the launch traced here: 69.1 us
  Pallas kernels  63.5 us (92%)
  local copies, waits for them, and re-layouts  4.76 us (7%)
  other arithmetic  0.76 us (1%)
    pallas_call x1, Pallas kernels, operator_kernel(): pl.pallas_call(functools.partial(project_kernel, planes, chips, branches)...  63.5 us
    unnamed x7, local copies, waits for them, and re-layouts  3.96 us

profile of v4, /device:TPU:20, one launch (start us, length us, event | category | flops | bytes accessed | tf_op | source)
XLA Modules:
  0.0 69.1 jit_solution(17791447864283737663)
XLA Ops:
  0.0 0.7 broadcast_in_dim.3
  0.7 0.8 %fusion.1 = f32[3,64,4]{1,2,0:T(4,128)S(1)} fusion(s32[]{:T(128)S(6)} %select_n.3, f32[3,1,512]{2,1,0:T(1,128)S(1)} %broadcast_in_dim.3, f32[3,3,512]{2,1,0:T(4,128)} %param.9), kind=kLoop, calls=%fused_computation.3 | loop fusion | flops 768 | bytes 27652 | tf_op jit(solution)/shard_map/transpose | solution.py:551
  1.5 0.1 copy.8
  1.6 0.0 copy-start
  1.6 1.4 %copy-done = bf16[512,3,512]{2,0,1:T(8,128)(2,1)S(1)} copy-done((bf16[512,3,512]{2,0,1:T(8,128)(2,1)S(1)}, bf16[512,3,512]{2,0,1:T(8,128)(2,1)}, u32[]{:S(2)}) %copy-start) | copy-done | bytes 1572888
  3.0 0.0 copy-start.1
  3.0 0.9 %copy-done.1 = bf16[128,1024]{1,0:T(8,128)(2,1)S(1)} copy-done((bf16[128,1024]{1,0:T(8,128)(2,1)S(1)}, bf16[128,1024]{1,0:T(8,128)(2,1)}, u32[]{:S(2)}) %copy-start.1) | copy-done | bytes 262168
  3.9 0.0 copy-start.2
  3.9 0.9 %copy-done.2 = f32[64,1024]{1,0:T(8,128)S(1)} copy-done((f32[64,1024]{1,0:T(8,128)S(1)}, f32[64,1024]{1,0:T(8,128)}, u32[]{:S(2)}) %copy-start.2) | copy-done | bytes 262168
  4.9 63.5 %shard_map.73 = bf16[128,512]{1,0:T(8,128)(2,1)S(1)} custom-call(bf16[128,1024]{1,0:T(8,128)(2,1)S(1)} %copy-done.1, bf16[3,512,512]{2,1,0:T(8,128)(2,1)S(1)} %bitcast.4, f32[192,4]{1,0:T(8,128)S(1)} %bitcast.5, f32[64,1024]{1,0:T(8,128)S(1)} %copy-done.2, bf16[2048,1024]{1,0:T(8,128)(2,1)} %constant.16.clone.high_table, ...), custom_call_target="tpu_custom_call" | custom-call | tf_op jit(solution)/shard_map/pallas_call | solution.py:499
  68.4 0.7 copy.10
Async XLA Ops:
  1.6 1.4 %copy-start = (bf16[512,3,512]{2,0,1:T(8,128)(2,1)S(1)}, bf16[512,3,512]{2,0,1:T(8,128)(2,1)}, u32[]{:S(2)}) copy-start(bf16[512,3,512]{2,0,1:T(8,128)(2,1)} %param.8) | copy-start | bytes 4718596
  3.0 0.9 %copy-start.1 = (bf16[128,1024]{1,0:T(8,128)(2,1)S(1)}, bf16[128,1024]{1,0:T(8,128)(2,1)}, u32[]{:S(2)}) copy-start(bf16[128,1024]{1,0:T(8,128)(2,1)} %tokens.1) | copy-start | bytes 786436
  3.9 0.9 %copy-start.2 = (f32[64,1024]{1,0:T(8,128)S(1)}, f32[64,1024]{1,0:T(8,128)}, u32[]{:S(2)}) copy-start(f32[64,1024]{1,0:T(8,128)} %kernel.1) | copy-start | bytes 786436
